TPU v7x, 32 devices: a whole 2x2x4 slice. The times are simulated.
32 devices in a mesh: groups: 2 (over y), dp: 4 (over x, core), mp: 4 (over z).
Axes of the slice: x: 2, y: 2, z: 4, core: 2. Of those that a mesh axis runs over, the one named last changes fastest.
Arguments:
- activations: bfloat16 [16384, 8192], P(('groups', 'dp'), 'mp'), parts along dimension 0, may hold values from -6 to 6
- output_grads: bfloat16 [16384, 28672], P(('groups', 'dp'), 'mp'), parts along dimension 0, may hold values from -6 to 6
- grad_factors: bfloat16 [28672, 512], P('mp', 'dp'), may hold values from -0.03125 to 0.03125
- act_factors: bfloat16 [8192, 512], P('mp', 'dp'), may hold values from -0.0625 to 0.0625
Outputs:
- scores: float32 [8, 16], P(('groups', 'dp')), parts along dimension 0
There are 2 independent parts, one for each index of `groups`. A program takes and returns all parts, laid end to end along the dimension named above; an argument that names none is the same for every part. Nothing has to cross between parts.
All inputs are finite; a program needn't handle non-finite values.
Results may differ from a plain program's by a relative error of at most 0.015.
Values may be sent and summed in bfloat16 or wider, within the bound.
A program may use at most 128 MiB of HBM per device.

v0:
```python
import jax
import jax.numpy as jnp
from jax import lax
from jax.sharding import PartitionSpec as P

QUERIES = 16
RANK = 32
SEQ_LEN = 2048
SEQ_DEV = 1


def body(activations, output_grads, grad_factors, act_factors):
    full_grad, full_act = (
        lax.all_gather(grad_factors, "dp", axis=1, tiled=True),
        lax.all_gather(act_factors, "dp", axis=1, tiled=True),
    )
    tok_rows = activations.shape[0]
    columns = full_grad.shape[1]
    parts = lax.axis_size("mp")
    position = lax.axis_index("mp")
    seq_ids = jnp.arange(SEQ_DEV, dtype=jnp.int32)
    owned = tok_rows // parts
    grad_term = jnp.dot(output_grads, full_grad, preferred_element_type=jnp.float32)
    act_term = jnp.dot(activations, full_act, preferred_element_type=jnp.float32)
    summed = lax.psum_scatter(
        jnp.concatenate([grad_term, act_term], axis=1).astype(jnp.bfloat16),
        "mp",
        scatter_dimension=0,
        tiled=True,
    ).astype(jnp.float32)
    product = summed[:, :columns] * summed[:, columns:]
    token_scores = product.reshape(owned, QUERIES, RANK).sum(axis=2)
    row_seq = (position * owned + jnp.arange(owned, dtype=jnp.int32)) // SEQ_LEN
    member = (seq_ids[:, None] == row_seq[None, :]).astype(jnp.float32)
    partial_value = jnp.dot(member, token_scores, precision=lax.Precision.HIGHEST)
    totals = lax.psum(partial_value, "mp")
    return totals / jnp.sqrt(jnp.float32(SEQ_LEN * RANK))


def solution(mesh):
    return jax.shard_map(
        body,
        mesh=mesh,
        in_specs=(
            P(("groups", "dp"), "mp"),
            P(("groups", "dp"), "mp"),
            P("mp", "dp"),
            P("mp", "dp"),
        ),
        out_specs=P(("groups", "dp"), None),
        check_vma=False,
    )
```

profile of v0, /device:TPU:0, one launch (start us, length us, event | category | flops | bytes accessed | tf_op | source)
XLA Modules:
  0.0 212.4 jit_solution(11316051662339359055)
XLA Ops:
  6.5 0.0 all-gather.5.cloned.1.call-start
  6.5 0.7 all-gather.5.cloned.1.call-update
  7.3 0.0 all-gather.3.cloned.1.call-start
  7.3 0.7 all-gather.3.cloned.1.call-update
  8.0 0.0 reduce-scatter.2.cloned.1.call-start
  8.1 26.4 %all-gather.5.cloned.1.call-done = bf16[2048,512]{1,0:T(8,128)(2,1)} async-done(((bf16[2048,128]{1,0:T(8,128)(2,1)}), bf16[2048,512]{1,0:T(8,128)(2,1)}) %all-gather.5.cloned.1.call-update) | async-done | bytes 2097168 | tf_op jit(solution)/shard_map/all_gather | solution.py:15
  34.5 8.6 %convolution_convert_fusion.1 = bf16[2048,512]{0,1:T(8,128)(2,1)S(1)} fusion(bf16[2048,2048]{1,0:T(8,128)(2,1)} %param.4, bf16[2048,512]{1,0:T(8,128)(2,1)} %all-gather.5.cloned.1.call-done), kind=kOutput, calls=%fused_computation.2 | convolution fusion | flops 4296015872 | bytes 12582912 | tf_op jit(solution)/shard_map/dot_general | solution.py:24
  43.0 46.3 %all-gather.3.cloned.1.call-done = bf16[7168,512]{1,0:T(8,128)(2,1)} async-done(((bf16[7168,128]{1,0:T(8,128)(2,1)}), bf16[7168,512]{1,0:T(8,128)(2,1)}) %all-gather.3.cloned.1.call-update) | async-done | bytes 7340048 | tf_op jit(solution)/shard_map/all_gather | solution.py:14
  89.4 22.1 %convolution_convert_fusion = bf16[2048,512]{0,1:T(8,128)(2,1)} fusion(bf16[2048,7168]{1,0:T(8,128)(2,1)} %param.5, bf16[7168,512]{1,0:T(8,128)(2,1)} %all-gather.3.cloned.1.call-done), kind=kOutput, calls=%fused_computation.1 | convolution fusion | flops 15033434112 | bytes 38797312 | tf_op jit(solution)/shard_map/dot_general | solution.py:23
  111.5 4.1 %pad_maximum_fusion = bf16[2048,1024]{0,1:T(8,128)(2,1)} fusion(bf16[2048,512]{0,1:T(8,128)(2,1)S(1)} %convolution_convert_fusion.1, bf16[2048,512]{0,1:T(8,128)(2,1)} %convolution_convert_fusion), kind=kLoop, calls=%fused_computation | loop fusion | flops 8388608 | bytes 8388608 | tf_op jit(solution)/shard_map/concatenate | solution.py:26
  115.5 0.0 reduce-scatter.2.cloned.1.call-update
  115.6 76.9 %reduce-scatter.2.cloned.1.call-done = bf16[512,1024]{0,1:T(8,128)(2,1)} async-done(((bf16[2048,1024]{0,1:T(8,128)(2,1)}), bf16[512,1024]{0,1:T(8,128)(2,1)}) %reduce-scatter.2.cloned.1.call-update) | async-done | bytes 1048592 | tf_op jit(solution)/shard_map/reduce_scatter | solution.py:25
  192.5 1.5 convert_element_type.2
  194.0 0.3 bitcast_reduce_fusion
  194.3 0.1 fusion.4
  194.4 10.9 %psum.7 = f32[1,16]{1,0:T(1,128)S(1)} all-reduce(f32[1,16]{1,0:T(1,128)S(1)} %fusion.4), channel_id=1, replica_groups=mesh['groups'=2,'dp'=4,'mp'=4] {'mp'}, use_global_device_ids=true, to_apply=%region_2.3 | all-reduce | flops 16 | bytes 128 | tf_op jit(solution)/shard_map/psum | solution.py:36
  205.3 0.5 broadcast_multiply_fusion
  (2 shorter events, 0.0 us)
Async XLA Ops:
  6.5 27.9 %all-gather.5.cloned.1.call-start = ((), (), s32[]{:S(2)}) async-start(), calls=%async_computation.2 | async-start | bytes 2621440 | tf_op jit(solution)/shard_map/all_gather | solution.py:15
  7.3 82.1 %all-gather.3.cloned.1.call-start = ((), (), s32[]{:S(2)}) async-start(), calls=%async_computation.1 | async-start | bytes 9175040 | tf_op jit(solution)/shard_map/all_gather | solution.py:14
  8.0 184.5 %reduce-scatter.2.cloned.1.call-start = ((), (), s32[]{:S(2)}) async-start(), calls=%async_computation.3 | async-start | bytes 5242880 | tf_op jit(solution)/shard_map/reduce_scatter | solution.py:25
Sparse Core Ops, SparseCore 0:
  8.9 25.5 all-gather.4
  36.0 53.3 all-gather.2
  115.7 76.7 reduce-scatter.1
where the time goes:
time: 213 us; the launch traced here: 212 us
  waiting for transfers between devices  151 us (71%)
  matrix products  30.8 us (14%)
  between operations  13.1 us (6%)
  blocking collectives  10.9 us (5%)
  other arithmetic  6.38 us (3%)
    reduce_scatter x1, waiting for transfers between devices, body(): lax.psum_scatter(jnp.concatenate([grad_term, act_term], axis=1).astype(jn...  76.9 us
    all_gather x1, waiting for transfers between devices, body(): lax.all_gather(grad_factors, 'dp', axis=1, tiled=True)  46.3 us
    all_gather x1, waiting for transfers between devices, body(): lax.all_gather(act_factors, 'dp', axis=1, tiled=True)  26.4 us
    dot_general x1, matrix products, body(): jnp.dot(output_grads, full_grad, preferred_element_type=jnp.float32)  22.1 us
    psum x1, blocking collectives, body(): totals = lax.psum(partial_value, 'mp')  10.9 us
    dot_general x1, matrix products, body(): jnp.dot(activations, full_act, preferred_element_type=jnp.float32)  8.56 us
  transfers between devices with their start and end apart: 3, of which 3 were waited for; matrix products, arithmetic and copies ran while one was open for 4% of the time, Pallas kernels for 0%

commit v1 on v0

--- a/solution.py
+++ b/solution.py
@@ -1,6 +1,10 @@
+import functools
+
 import jax
 import jax.numpy as jnp
 from jax import lax
+from jax.experimental import pallas as pl
+from jax.experimental.pallas import tpu as pltpu
 from jax.sharding import PartitionSpec as P
 
 QUERIES = 16
@@ -8,8 +12,13 @@
 SEQ_LEN = 2048
 SEQ_DEV = 1
 
-
-def body(activations, output_grads, grad_factors, act_factors):
+BLOCKS = 8
+PIECES = 7
+OG_SLOTS = 3
+MESH = pl.DeviceIdType.MESH
+
+
+def plain_body(activations, output_grads, grad_factors, act_factors):
     full_grad, full_act = (
         lax.all_gather(grad_factors, "dp", axis=1, tiled=True),
         lax.all_gather(act_factors, "dp", axis=1, tiled=True),
@@ -37,7 +46,339 @@
     return totals / jnp.sqrt(jnp.float32(SEQ_LEN * RANK))
 
 
+def kernel(
+    n,
+    act, og, gf, af, out,
+    act_v, og_v, fa, fg, own_a, g_v, tmp, acc, gath,
+    p_send, p_recv, s_send, s_recv,
+    load_act, load_f, load_og,
+    sib_s, sib_r, xs, xr, ys, yr, sxs, sxr, sys_, syr,
+    pss, prs, sss, srs, fs, fr,
+):
+    g = lax.axis_index("groups")
+    d = lax.axis_index("dp")
+    z = lax.axis_index("mp")
+    core = lax.rem(d, 2)
+    x = d // 2
+    sib = (g, d + 1 - 2 * core, z)
+    xn = (g, lax.rem(d + 2, 4), z)
+    yn = (1 - g, d, z)
+    rows = act.shape[0] // BLOCKS
+    w = gf.shape[1]
+    ka, kg = af.shape[0] // 2, gf.shape[0] // 2
+    kp = kg // PIECES
+    chunks = 2 * BLOCKS
+    cols = pl.ds(pl.multiple_of(core * w, w), w)
+
+    def act_load(b):
+        r = pl.ds(pl.multiple_of(b * rows, rows), rows)
+        return pltpu.make_async_copy(act.at[r], act_v.at[r], load_act.at[b])
+
+    def og_load(j):
+        r = pl.ds(pl.multiple_of(lax.rem(j, BLOCKS) * rows, rows), rows)
+        slot = lax.rem(j, OG_SLOTS)
+        return pltpu.make_async_copy(og.at[r], og_v.at[slot], load_og.at[slot])
+
+    def remote(src, dst, ss, rs, dev):
+        return pltpu.make_async_remote_copy(
+            src_ref=src, dst_ref=dst, send_sem=ss, recv_sem=rs,
+            device_id=dev, device_id_type=MESH,
+        )
+
+    def arows(side):
+        return pl.ds(pl.multiple_of(side * ka, ka), ka)
+
+    def grows(side, k):
+        return pl.ds(pl.multiple_of(side * kg + k * kp, kp), kp)
+
+    load_fa = pltpu.make_async_copy(af, fa.at[0, :, cols], load_f.at[0])
+    load_fg = pltpu.make_async_copy(gf, fg.at[0, :, cols], load_f.at[1])
+    sib_a = remote(af, fa.at[0, :, cols], sib_s.at[0], sib_r.at[0], sib)
+    sib_g = remote(gf, fg.at[0, :, cols], sib_s.at[1], sib_r.at[1], sib)
+
+    def x_a():
+        return remote(af.at[arows(g)], fa.at[1, arows(g), cols], xs.at[0], xr.at[0], xn)
+
+    def x_g(k):
+        return remote(gf.at[grows(g, k)], fg.at[1, grows(g, k), cols], xs.at[k + 1], xr.at[k + 1], xn)
+
+    def fwd_a(side, ss, rs, dev):
+        ref = fa.at[1, arows(side), cols]
+        return remote(ref, ref, ss.at[0], rs.at[0], dev)
+
+    def fwd_g(side, k, ss, rs, dev):
+        ref = fg.at[1, grows(side, k), cols]
+        return remote(ref, ref, ss.at[k + 1], rs.at[k + 1], dev)
+
+    load_fa.start()
+    for b in range(BLOCKS):
+        act_load(b).start()
+    load_fg.start()
+    for j in range(OG_SLOTS):
+        og_load(j).start()
+    acc[...] = jnp.zeros_like(acc)
+
+    barrier = pltpu.get_barrier_semaphore()
+    for dev in (sib, xn, yn):
+        pl.semaphore_signal(barrier, inc=1, device_id=dev, device_id_type=MESH)
+    for o in range(1, n):
+        pl.semaphore_signal(
+            barrier, inc=1, device_id=(g, d, lax.rem(z + o, n)), device_id_type=MESH
+        )
+    pl.semaphore_wait(barrier, 3 + n - 1)
+
+    sib_a.start()
+    x_a().start()
+    for k in range(PIECES):
+        x_g(k).start()
+    sib_g.start()
+    load_fa.wait()
+    sib_a.wait_recv()
+
+    def p_copy(c):
+        return remote(p_send.at[c], p_recv.at[c], pss.at[c], prs.at[c], (g, d, lax.rem(z + 1, n)))
+
+    def s_copy(c):
+        return remote(s_send.at[c], s_recv.at[c], sss.at[c], srs.at[c], (g, d, lax.rem(z + n - 1, n)))
+
+    def relay(c, first, last, copy, send, recv):
+        @pl.when((c >= 0) & (c < chunks))
+        def _():
+            @pl.when(jnp.logical_not(first))
+            def _():
+                copy(c).wait_recv()
+
+                @pl.when(jnp.logical_not(last))
+                def _():
+                    send[c] = (own_a[c] + recv[c].astype(jnp.float32)).astype(jnp.bfloat16)
+
+            @pl.when(first)
+            def _():
+                send[c] = own_a[c].astype(jnp.bfloat16)
+
+            @pl.when(jnp.logical_not(last))
+            def _():
+                copy(c).start()
+
+    h1_step = 12
+
+    def step(s, carry):
+        @pl.when(s < BLOCKS)
+        def _():
+            act_load(s).wait()
+
+        @pl.when(s == BLOCKS)
+        def _():
+            fwd_a(g, sxs, sxr, sib).wait_recv()
+            fwd_a(1 - g, sys_, syr, sib).wait_recv()
+
+        @pl.when(s < chunks)
+        def _():
+            b = lax.rem(s, BLOCKS)
+            r = pl.ds(pl.multiple_of(b * rows, rows), rows)
+            own_a[s] = jnp.dot(
+                act_v[r, :], fa[s // BLOCKS], preferred_element_type=jnp.float32
+            )
+
+        relay(s - z, z == 0, z == n - 1, p_copy, p_send, p_recv)
+        relay(s - (n - 1 - z), z == n - 1, z == 0, s_copy, s_send, s_recv)
+
+        @pl.when(s == 2)
+        def _():
+            x_a().wait_recv()
+            fwd_a(g, ys, yr, yn).start()
+            fwd_a(g, sxs, sxr, sib).start()
+
+        @pl.when((s >= 3) & (s < 3 + PIECES))
+        def _():
+            k = s - 3
+            x_g(k).wait_recv()
+            fwd_g(g, k, ys, yr, yn).start()
+            fwd_g(g, k, sxs, sxr, sib).start()
+
+        @pl.when(s == 4)
+        def _():
+            fwd_a(1 - g, ys, yr, yn).wait_recv()
+            fwd_a(1 - g, sys_, syr, sib).start()
+
+        @pl.when((s >= 5) & (s < 5 + PIECES))
+        def _():
+            k = s - 5
+            fwd_g(1 - g, k, ys, yr, yn).wait_recv()
+            fwd_g(1 - g, k, sys_, syr, sib).start()
+
+        @pl.when(s == 2)
+        def _():
+            load_fg.wait()
+            sib_g.wait_recv()
+
+        @pl.when(s == h1_step)
+        def _():
+            def got(k, carry):
+                fwd_g(g, k, sxs, sxr, sib).wait_recv()
+                fwd_g(1 - g, k, sys_, syr, sib).wait_recv()
+                return carry
+
+            lax.fori_loop(0, PIECES, got, 0)
+
+        early = (s >= 2) & (s < 2 + BLOCKS)
+        late = (s >= h1_step) & (s < h1_step + BLOCKS // 2)
+        first = jnp.where(early, s - 2, BLOCKS + 2 * (s - h1_step))
+        count = jnp.where(early, 1, jnp.where(late, 2, 0))
+
+        def grad_block(i, carry):
+            j = first + i
+            og_load(j).wait()
+            g_v[j] = jnp.dot(
+                og_v[lax.rem(j, OG_SLOTS)], fg[j // BLOCKS],
+                preferred_element_type=jnp.float32,
+            )
+
+            @pl.when(j + OG_SLOTS < chunks)
+            def _():
+                og_load(j + OG_SLOTS).start()
+
+            return carry
+
+        lax.fori_loop(0, count, grad_block, 0)
+
+        c = s - n
+
+        @pl.when(c >= 0)
+        def _():
+            tmp[...] = own_a[c]
+
+            @pl.when(z > 0)
+            def _():
+                tmp[...] += p_recv[c].astype(jnp.float32)
+
+            @pl.when(z < n - 1)
+            def _():
+                tmp[...] += s_recv[c].astype(jnp.float32)
+
+            prod = (tmp[...] * g_v[c]).reshape(rows // 8, 8, 2 * w).sum(axis=0)
+            half = c // BLOCKS
+            place = half + x - 2 * half * x
+            at = pl.ds(pl.multiple_of(place * 2 * w, 2 * w), 2 * w)
+            acc[:, at] += prod
+
+        return carry
+
+    lax.fori_loop(0, chunks + n, step, 0)
+
+    gath[z] = acc[...]
+
+    def final(o):
+        return remote(acc, gath.at[z], fs.at[o], fr.at[o], (g, d, lax.rem(z + o, n)))
+
+    def final_in(o):
+        src = lax.rem(z + n - o, n)
+        return remote(acc, gath.at[src], fs.at[o], fr.at[o], (g, d, src))
+
+    for o in range(1, n):
+        final(o).start()
+
+    sib_a.wait_send()
+    sib_g.wait_send()
+    x_a().wait_send()
+    fwd_a(g, ys, yr, yn).wait_send()
+    fwd_a(g, sxs, sxr, sib).wait_send()
+    fwd_a(1 - g, sys_, syr, sib).wait_send()
+
+    def sent(k, carry):
+        x_g(k).wait_send()
+        fwd_g(g, k, ys, yr, yn).wait_send()
+        fwd_g(g, k, sxs, sxr, sib).wait_send()
+        fwd_g(1 - g, k, sys_, syr, sib).wait_send()
+        return carry
+
+    lax.fori_loop(0, PIECES, sent, 0)
+
+    @pl.when(z < n - 1)
+    def _():
+        def sent_p(c, carry):
+            p_copy(c).wait_send()
+            return carry
+
+        lax.fori_loop(0, chunks, sent_p, 0)
+
+    @pl.when(z > 0)
+    def _():
+        def sent_s(c, carry):
+            s_copy(c).wait_send()
+            return carry
+
+        lax.fori_loop(0, chunks, sent_s, 0)
+
+    for o in range(1, n):
+        final_in(o).wait_recv()
+    for o in range(1, n):
+        final(o).wait_send()
+    total = gath[0]
+    for i in range(1, n):
+        total = total + gath[i]
+    out[...] = total
+
+
+def kernel_body(n, activations, output_grads, grad_factors, act_factors):
+    tokens, ka = activations.shape
+    kg, w = grad_factors.shape
+    rows = tokens // BLOCKS
+    chunks = 2 * BLOCKS
+    bf, f32 = jnp.bfloat16, jnp.float32
+    dma = pltpu.SemaphoreType.DMA
+    block = (chunks, rows, 2 * w)
+    total = pl.pallas_call(
+        functools.partial(kernel, n),
+        out_shape=jax.ShapeDtypeStruct((8, 4 * w), f32),
+        in_specs=[pl.BlockSpec(memory_space=pl.ANY)] * 4,
+        out_specs=pl.BlockSpec(memory_space=pltpu.VMEM),
+        scratch_shapes=[
+            pltpu.VMEM((tokens, ka), bf),
+            pltpu.VMEM((OG_SLOTS, rows, kg), bf),
+            pltpu.VMEM((2, ka, 2 * w), bf),
+            pltpu.VMEM((2, kg, 2 * w), bf),
+            pltpu.VMEM(block, f32),
+            pltpu.VMEM(block, f32),
+            pltpu.VMEM((rows, 2 * w), f32),
+            pltpu.VMEM((8, 4 * w), f32),
+            pltpu.VMEM((n, 8, 4 * w), f32),
+        ]
+        + [pltpu.VMEM(block, bf)] * 4
+        + [dma((BLOCKS,)), dma((2,)), dma((OG_SLOTS,)), dma((2,)), dma((2,))]
+        + [dma((PIECES + 1,))] * 8
+        + [dma((chunks,))] * 4
+        + [dma((n,))] * 2,
+        compiler_params=pltpu.CompilerParams(
+            collective_id=0, has_side_effects=True, vmem_limit_bytes=58 * 2**20
+        ),
+        cost_estimate=pl.CostEstimate(
+            flops=2 * tokens * (ka + kg) * 4 * w,
+            bytes_accessed=2 * tokens * (ka + 2 * kg),
+            transcendentals=0,
+        ),
+    )(activations, output_grads, grad_factors, act_factors)
+    scores = total.sum(axis=0).reshape(QUERIES, RANK).sum(axis=1)
+    return scores[None, :] / jnp.sqrt(jnp.float32(SEQ_LEN * RANK))
+
+
 def solution(mesh):
+    shape = dict(mesh.shape)
+
+    def body(activations, output_grads, grad_factors, act_factors):
+        kg, w = grad_factors.shape
+        fits = (
+            shape["groups"] == 2
+            and shape["dp"] == 4
+            and 4 <= shape["mp"] <= 7
+            and w == 128
+            and activations.shape[0] == SEQ_LEN
+            and activations.shape[1] % 32 == 0
+            and kg % (32 * PIECES) == 0
+        )
+        run = functools.partial(kernel_body, shape["mp"]) if fits else plain_body
+        return run(activations, output_grads, grad_factors, act_factors)
+
     return jax.shard_map(
         body,
         mesh=mesh,

time: 213 us -> 91.4 us (0.43)
  waiting for transfers between devices: 151 us -> 0 us
  Pallas kernels: 0 us -> 89.7 us
  matrix products: 30.8 us -> 0 us
  between operations: 13.1 us -> 0.01 us
  blocking collectives: 10.9 us -> 0 us
  other arithmetic: 6.38 us -> 1.37 us
    pallas_call x0 -> x1, Pallas kernels: none -> 89.7 us  [kernel_body(): pl.pallas_call(functools.partial(kernel, n), out_shape=jax.ShapeDtypeStru...]
    reduce_scatter x1 -> x0, waiting for transfers between devices: 76.9 us -> none  [body(): lax.psum_scatter(jnp.concatenate([grad_term, act_term], axis=1).astype(jn...]
    all_gather x2 -> x0, waiting for transfers between devices: 72.8 us -> none  [the longest x1 46.3 us: body(): lax.all_gather(grad_factors, 'dp', axis=1, tiled=True)]
    dot_general x3 -> x0, matrix products: 30.8 us -> none  [the longest x1 22.1 us: body(): jnp.dot(output_grads, full_grad, preferred_element_type=jnp.float32)]
    psum x1 -> x0, blocking collectives: 10.9 us -> none  [body(): totals = lax.psum(partial_value, 'mp')]
    concatenate x1 -> x0, other arithmetic: 4.06 us -> none  [body(): jnp.concatenate([grad_term, act_term], axis=1).astype(jnp.bfloat16)]
  transfers between devices with their start and end apart: 3 -> 0, of which waited for: 3 -> 0; matrix products, arithmetic and copies ran while one was open for 4% -> 0% of each run, Pallas kernels for 0% -> 0%
where the time goes in v1:
time: 91.4 us; the launch traced here: 91.1 us
  Pallas kernels  89.7 us (98%)
  other arithmetic  1.37 us (1%)
    pallas_call x1, Pallas kernels, kernel_body(): pl.pallas_call(functools.partial(kernel, n), out_shape=jax.ShapeDtypeStru...  89.7 us

profile of v1, /device:TPU:0, one launch (start us, length us, event | category | flops | bytes accessed | tf_op | source)
XLA Modules:
  0.0 91.1 jit_solution(5567258655948863359)
XLA Ops:
  0.0 89.7 %shard_map.46 = f32[8,512]{1,0:T(8,128)} custom-call(bf16[2048,2048]{1,0:T(8,128)(2,1)} %act.1, bf16[2048,7168]{1,0:T(8,128)(2,1)} %og.1, bf16[7168,128]{1,0:T(8,128)(2,1)} %gf.1, bf16[2048,128]{1,0:T(8,128)(2,1)} %af.1), custom_call_target="tpu_custom_call" | custom-call | flops 19327352832 | bytes 67108864 | tf_op jit(solution)/shard_map/pallas_call | solution.py:331
  89.7 0.7 reduce_sum.18
  90.4 0.1 reshape.13
  90.5 0.1 reduce_sum.19
  90.6 0.5 multiply_bitcast_fusion

commit v2 on v1

--- a/solution.py
+++ b/solution.py
@@ -13,8 +13,12 @@
 SEQ_DEV = 1
 
 BLOCKS = 8
-PIECES = 7
+SUB = 2
+SKEW = 3
+GROUP = 1
+PIECES = 14
 OG_SLOTS = 3
+X_FIRST, Y_FIRST, X_EVERY = 3, 7, 1
 MESH = pl.DeviceIdType.MESH
 
 
@@ -67,7 +71,11 @@
     w = gf.shape[1]
     ka, kg = af.shape[0] // 2, gf.shape[0] // 2
     kp = kg // PIECES
-    chunks = 2 * BLOCKS
+    sub = rows // SUB
+    chunks = 2 * BLOCKS * SUB
+    lag = SKEW * (n - 1) + 1
+    per = SUB * GROUP
+    gblocks = BLOCKS // GROUP
     cols = pl.ds(pl.multiple_of(core * w, w), w)
 
     def act_load(b):
@@ -75,7 +83,8 @@
         return pltpu.make_async_copy(act.at[r], act_v.at[r], load_act.at[b])
 
     def og_load(j):
-        r = pl.ds(pl.multiple_of(lax.rem(j, BLOCKS) * rows, rows), rows)
+        m = rows * GROUP
+        r = pl.ds(pl.multiple_of(lax.rem(j, gblocks) * m, m), m)
         slot = lax.rem(j, OG_SLOTS)
         return pltpu.make_async_copy(og.at[r], og_v.at[slot], load_og.at[slot])
 
@@ -111,11 +120,7 @@
         return remote(ref, ref, ss.at[k + 1], rs.at[k + 1], dev)
 
     load_fa.start()
-    for b in range(BLOCKS):
-        act_load(b).start()
-    load_fg.start()
-    for j in range(OG_SLOTS):
-        og_load(j).start()
+    act_load(0).start()
     acc[...] = jnp.zeros_like(acc)
 
     barrier = pltpu.get_barrier_semaphore()
@@ -132,6 +137,8 @@
     for k in range(PIECES):
         x_g(k).start()
     sib_g.start()
+    for b in range(1, BLOCKS):
+        act_load(b).start()
     load_fa.wait()
     sib_a.wait_recv()
 
@@ -160,59 +167,71 @@
             def _():
                 copy(c).start()
 
-    h1_step = 12
-
     def step(s, carry):
-        @pl.when(s < BLOCKS)
-        def _():
-            act_load(s).wait()
-
-        @pl.when(s == BLOCKS)
+        b = s // SUB
+        block_start = lax.rem(s, SUB) == 0
+
+        @pl.when(block_start & (b < BLOCKS))
+        def _():
+            act_load(b).wait()
+
+        @pl.when(s == BLOCKS * SUB)
         def _():
             fwd_a(g, sxs, sxr, sib).wait_recv()
             fwd_a(1 - g, sys_, syr, sib).wait_recv()
 
-        @pl.when(s < chunks)
-        def _():
-            b = lax.rem(s, BLOCKS)
-            r = pl.ds(pl.multiple_of(b * rows, rows), rows)
-            own_a[s] = jnp.dot(
-                act_v[r, :], fa[s // BLOCKS], preferred_element_type=jnp.float32
-            )
-
-        relay(s - z, z == 0, z == n - 1, p_copy, p_send, p_recv)
-        relay(s - (n - 1 - z), z == n - 1, z == 0, s_copy, s_send, s_recv)
+        @pl.when(block_start & (s < chunks))
+        def _():
+            r = pl.ds(pl.multiple_of(lax.rem(b, BLOCKS) * rows, rows), rows)
+            own_a[pl.ds(pl.multiple_of(b * SUB, SUB), SUB)] = jnp.dot(
+                act_v[r, :], fa[b // BLOCKS], preferred_element_type=jnp.float32
+            ).reshape(SUB, sub, 2 * w)
+
+        relay(s - SKEW * z, z == 0, z == n - 1, p_copy, p_send, p_recv)
+        relay(s - SKEW * (n - 1 - z), z == n - 1, z == 0, s_copy, s_send, s_recv)
 
         @pl.when(s == 2)
+        def _():
+            load_fg.start()
+            for j in range(OG_SLOTS):
+                og_load(j).start()
+
+        @pl.when(s == X_FIRST)
         def _():
             x_a().wait_recv()
             fwd_a(g, ys, yr, yn).start()
             fwd_a(g, sxs, sxr, sib).start()
 
-        @pl.when((s >= 3) & (s < 3 + PIECES))
-        def _():
-            k = s - 3
+        u = s - (X_FIRST + X_EVERY)
+
+        @pl.when((u >= 0) & (u < X_EVERY * PIECES) & (lax.rem(s + X_EVERY * X_FIRST - X_FIRST, X_EVERY) == 0))
+        def _():
+            k = u // X_EVERY
             x_g(k).wait_recv()
             fwd_g(g, k, ys, yr, yn).start()
             fwd_g(g, k, sxs, sxr, sib).start()
 
-        @pl.when(s == 4)
+        @pl.when(s == Y_FIRST)
         def _():
             fwd_a(1 - g, ys, yr, yn).wait_recv()
             fwd_a(1 - g, sys_, syr, sib).start()
 
-        @pl.when((s >= 5) & (s < 5 + PIECES))
-        def _():
-            k = s - 5
+        v = s - (Y_FIRST + X_EVERY)
+
+        @pl.when((v >= 0) & (v < X_EVERY * PIECES) & (lax.rem(s + X_EVERY * Y_FIRST - Y_FIRST, X_EVERY) == 0))
+        def _():
+            k = v // X_EVERY
             fwd_g(1 - g, k, ys, yr, yn).wait_recv()
             fwd_g(1 - g, k, sys_, syr, sib).start()
 
-        @pl.when(s == 2)
+        c = s - lag
+
+        @pl.when(c == 0)
         def _():
             load_fg.wait()
             sib_g.wait_recv()
 
-        @pl.when(s == h1_step)
+        @pl.when(c == BLOCKS * SUB)
         def _():
             def got(k, carry):
                 fwd_g(g, k, sxs, sxr, sib).wait_recv()
@@ -221,29 +240,19 @@
 
             lax.fori_loop(0, PIECES, got, 0)
 
-        early = (s >= 2) & (s < 2 + BLOCKS)
-        late = (s >= h1_step) & (s < h1_step + BLOCKS // 2)
-        first = jnp.where(early, s - 2, BLOCKS + 2 * (s - h1_step))
-        count = jnp.where(early, 1, jnp.where(late, 2, 0))
-
-        def grad_block(i, carry):
-            j = first + i
+        @pl.when((c >= 0) & (lax.rem(s + per * lag - lag, per) == 0))
+        def _():
+            j = c // per
             og_load(j).wait()
-            g_v[j] = jnp.dot(
-                og_v[lax.rem(j, OG_SLOTS)], fg[j // BLOCKS],
+            g_v[...] = jnp.dot(
+                og_v[lax.rem(j, OG_SLOTS)], fg[j // gblocks],
                 preferred_element_type=jnp.float32,
-            )
-
-            @pl.when(j + OG_SLOTS < chunks)
+            ).reshape(per, sub, 2 * w)
+
+            @pl.when(j + OG_SLOTS < 2 * gblocks)
             def _():
                 og_load(j + OG_SLOTS).start()
 
-            return carry
-
-        lax.fori_loop(0, count, grad_block, 0)
-
-        c = s - n
-
         @pl.when(c >= 0)
         def _():
             tmp[...] = own_a[c]
@@ -256,15 +265,15 @@
             def _():
                 tmp[...] += s_recv[c].astype(jnp.float32)
 
-            prod = (tmp[...] * g_v[c]).reshape(rows // 8, 8, 2 * w).sum(axis=0)
-            half = c // BLOCKS
+            prod = (tmp[...] * g_v[lax.rem(c, per)]).reshape(sub // 8, 8, 2 * w).sum(axis=0)
+            half = c // (BLOCKS * SUB)
             place = half + x - 2 * half * x
             at = pl.ds(pl.multiple_of(place * 2 * w, 2 * w), 2 * w)
             acc[:, at] += prod
 
         return carry
 
-    lax.fori_loop(0, chunks + n, step, 0)
+    lax.fori_loop(0, chunks + lag, step, 0)
 
     gath[z] = acc[...]
 
@@ -324,10 +333,10 @@
     tokens, ka = activations.shape
     kg, w = grad_factors.shape
     rows = tokens // BLOCKS
-    chunks = 2 * BLOCKS
+    chunks = 2 * BLOCKS * SUB
     bf, f32 = jnp.bfloat16, jnp.float32
     dma = pltpu.SemaphoreType.DMA
-    block = (chunks, rows, 2 * w)
+    block = (chunks, rows // SUB, 2 * w)
     total = pl.pallas_call(
         functools.partial(kernel, n),
         out_shape=jax.ShapeDtypeStruct((8, 4 * w), f32),
@@ -335,12 +344,12 @@
         out_specs=pl.BlockSpec(memory_space=pltpu.VMEM),
         scratch_shapes=[
             pltpu.VMEM((tokens, ka), bf),
-            pltpu.VMEM((OG_SLOTS, rows, kg), bf),
+            pltpu.VMEM((OG_SLOTS, GROUP * rows, kg), bf),
             pltpu.VMEM((2, ka, 2 * w), bf),
             pltpu.VMEM((2, kg, 2 * w), bf),
             pltpu.VMEM(block, f32),
-            pltpu.VMEM(block, f32),
-            pltpu.VMEM((rows, 2 * w), f32),
+            pltpu.VMEM((SUB * GROUP,) + block[1:], f32),
+            pltpu.VMEM(block[1:], f32),
             pltpu.VMEM((8, 4 * w), f32),
             pltpu.VMEM((n, 8, 4 * w), f32),
         ]

time: 91.4 us -> 76.2 us (0.83)
  Pallas kernels: 89.7 us -> 74.5 us
    pallas_call x1, Pallas kernels: 89.7 us -> 74.5 us  [kernel_body(): pl.pallas_call(functools.partial(kernel, n), out_shape=jax.ShapeDtypeStru...]
where the time goes in v2:
time: 76.2 us; the launch traced here: 76 us
  Pallas kernels  74.5 us (98%)
  other arithmetic  1.37 us (2%)
    pallas_call x1, Pallas kernels, kernel_body(): pl.pallas_call(functools.partial(kernel, n), out_shape=jax.ShapeDtypeStru...  74.5 us

profile of v2, /device:TPU:0, one launch (start us, length us, event | category | flops | bytes accessed | tf_op | source)
XLA Modules:
  0.0 76.0 jit_solution(16871729124220744654)
XLA Ops:
  0.0 74.5 %shard_map.46 = f32[8,512]{1,0:T(8,128)} custom-call(bf16[2048,2048]{1,0:T(8,128)(2,1)} %act.1, bf16[2048,7168]{1,0:T(8,128)(2,1)} %og.1, bf16[7168,128]{1,0:T(8,128)(2,1)} %gf.1, bf16[2048,128]{1,0:T(8,128)(2,1)} %af.1), custom_call_target="tpu_custom_call" | custom-call | flops 19327352832 | bytes 67108864 | tf_op jit(solution)/shard_map/pallas_call | solution.py:340
  74.6 0.7 reduce_sum.18
  75.3 0.1 reshape.13
  75.4 0.1 reduce_sum.19
  75.5 0.5 multiply_bitcast_fusion

commit v3 on v2

--- a/solution.py
+++ b/solution.py
@@ -18,7 +18,7 @@
 GROUP = 1
 PIECES = 14
 OG_SLOTS = 3
-X_FIRST, Y_FIRST, X_EVERY = 3, 7, 1
+X_FIRST, Y_FIRST, X_EVERY = 5, 9, 1
 MESH = pl.DeviceIdType.MESH
 
 

time: 76.2 us -> 74.1 us (0.972)
  Pallas kernels: 74.5 us -> 72.4 us
    pallas_call x1, Pallas kernels: 74.5 us -> 72.4 us  [kernel_body(): pl.pallas_call(functools.partial(kernel, n), out_shape=jax.ShapeDtypeStru...]
where the time goes in v3:
time: 74.1 us; the launch traced here: 73.9 us
  Pallas kernels  72.4 us (98%)
  other arithmetic  1.37 us (2%)
    pallas_call x1, Pallas kernels, kernel_body(): pl.pallas_call(functools.partial(kernel, n), out_shape=jax.ShapeDtypeStru...  72.4 us

profile of v3, /device:TPU:0, one launch (start us, length us, event | category | flops | bytes accessed | tf_op | source)
XLA Modules:
  0.0 73.9 jit_solution(7385321266596069793)
XLA Ops:
  0.0 72.4 %shard_map.46 = f32[8,512]{1,0:T(8,128)} custom-call(bf16[2048,2048]{1,0:T(8,128)(2,1)} %act.1, bf16[2048,7168]{1,0:T(8,128)(2,1)} %og.1, bf16[7168,128]{1,0:T(8,128)(2,1)} %gf.1, bf16[2048,128]{1,0:T(8,128)(2,1)} %af.1), custom_call_target="tpu_custom_call" | custom-call | flops 19327352832 | bytes 67108864 | tf_op jit(solution)/shard_map/pallas_call | solution.py:340
  72.5 0.7 reduce_sum.18
  73.2 0.1 reshape.13
  73.3 0.1 reduce_sum.19
  73.4 0.5 multiply_bitcast_fusion
